TPU v7x, 32 devices: a whole 2x2x4 slice. The times are simulated.
32 devices in a mesh: groups: 2 (over y), space: 4 (over z), tangent: 4 (over x, core).
Axes of the slice: x: 2, y: 2, z: 4, core: 2. Of those that a mesh axis runs over, the one named last changes fastest.
Arguments:
- positions: float32 [16, 2, 128], P(('groups', 'space')), parts along dimension 0, may hold values from 0.45 to 15.55, as said below
- momenta: float32 [16, 2, 128], P(('groups', 'space')), parts along dimension 0, may hold values from -4 to 4
- cell_count: int32 [16], P(('groups', 'space')), parts along dimension 0, may hold values from 64 to 128, as said below
- tangent: float32 [16, 4, 128, 1024], P(('groups', 'space'), None, None, 'tangent'), parts along dimension 0, may hold values from -6 to 6
Outputs:
- phase: float32 [16, 4, 128], P(('groups', 'space')), parts along dimension 0
- new_tangent: float32 [16, 4, 128, 1024], P(('groups', 'space'), None, None, 'tangent'), parts along dimension 0
- stretch: float32 [2048], P(('groups', 'tangent')), parts along dimension 0
There are 2 independent parts, one for each index of `groups`. A program takes and returns all parts, laid end to end along the dimension named above; each array names one. Nothing has to cross between parts.
Inputs may be any that keep to these rules, and one draw needn't show every extreme that they name: Slots 0 to cell_count - 1 of a cell hold particles, the others are padding; some cell holds 128 particles in every draw. `positions`: every slot of a cell, padding too, lies within 0.05 in each coordinate of its own point of the lattice (m + 0.5, n + 0.5), m from 0 to 7, n from 0 to 15; no two slots of a cell share a lattice point.
All inputs are finite; a program needn't handle non-finite values.
Results may differ from a plain program's by a relative error of at most 0.006.
Values may be sent and summed in bfloat16 or wider, within the bound.
No kernel may reach another device: no remote copies, remote signals or barrier semaphores. Data moves between devices by JAX's collectives and lax.ppermute only.
A program may use at most 128 MiB of HBM per device.

v0:
```python
import jax
import jax.numpy as jnp
from jax import lax
from jax.sharding import PartitionSpec as P

STEPS = 2
DT = 0.005
CUT2 = 2.0 ** (1.0 / 3.0)
PARK = 1000.0
HIGH = lax.Precision.HIGHEST


def padded(block, sides, width):
    for axis, dim in sides:
        count = lax.axis_size(axis)
        forward = [(i, i + 1) for i in range(count - 1)]
        forward.append((count - 1, 0))
        backward = [(target, source) for source, target in forward]
        low = lax.ppermute(
            lax.slice_in_dim(block, block.shape[dim] - width, None, axis=dim), axis, forward
        )
        high = lax.ppermute(lax.slice_in_dim(block, 0, width, axis=dim), axis, backward)
        block = jnp.concatenate([low, block, high], axis=dim)
    return block


def pair_terms(own_coords, own_alive, far_coords, shift_x, shift_y, same_cell):
    delta_x = shift_x + far_coords[:, 0, None, :] - own_coords[:, 0, :, None]
    delta_y = shift_y + far_coords[:, 1, None, :] - own_coords[:, 1, :, None]
    dist2 = delta_x * delta_x + delta_y * delta_y
    within = jnp.logical_and(dist2 < CUT2, own_alive[:, :, None] > 0.5)
    if same_cell:
        within = jnp.logical_and(within, jnp.logical_not(jnp.eye(dist2.shape[-1], dtype=bool)))
    weight = within.astype(jnp.float32)
    safe = jnp.where(within, dist2, CUT2)
    inverse = 1.0 / safe
    inv_three = inverse * inverse * inverse
    inv_six = inv_three * inv_three
    energy = 4.0 * (inv_six - inv_three) + 1.0
    energy_1 = 4.0 * (3.0 * inv_three - 6.0 * inv_six) * inverse
    energy_2 = 4.0 * (42.0 * inv_six - 12.0 * inv_three) * inverse * inverse
    taper = 1.0 - safe / CUT2
    switch = taper * taper
    switch_1 = -2.0 * taper / CUT2
    switch_2 = 2.0 / (CUT2 * CUT2)
    grad_1 = (energy_1 * switch + energy * switch_1) * weight
    grad_2 = (energy_2 * switch + 2.0 * energy_1 * switch_1 + energy * switch_2) * weight
    pull_x = 2.0 * grad_1 * delta_x
    pull_y = 2.0 * grad_1 * delta_y
    k_xx = (2.0 * grad_1 + 4.0 * grad_2 * delta_x * delta_x).astype(jnp.bfloat16)
    k_xy = (4.0 * grad_2 * delta_x * delta_y).astype(jnp.bfloat16)
    k_yy = (2.0 * grad_1 + 4.0 * grad_2 * delta_y * delta_y).astype(jnp.bfloat16)
    return (pull_x, pull_y, k_xx, k_xy, k_yy)


def apply_rows(k_xx, k_xy, k_yy, far_low):
    gain_x = jnp.einsum(
        "cij,cjv->civ", k_xx, far_low[:, 0], preferred_element_type=jnp.float32
    ) + jnp.einsum("cij,cjv->civ", k_xy, far_low[:, 1], preferred_element_type=jnp.float32)
    gain_y = jnp.einsum(
        "cij,cjv->civ", k_xy, far_low[:, 0], preferred_element_type=jnp.float32
    ) + jnp.einsum("cij,cjv->civ", k_yy, far_low[:, 1], preferred_element_type=jnp.float32)
    return (gain_x, gain_y)


def add_pair(totals, parked, occupied, far_coords, far_low, shift_x, shift_y, same_cell):
    forces_x, forces_y, push_x, push_y, diag_xx, diag_xy, diag_yy = totals
    pull_x, pull_y, k_xx, k_xy, k_yy = pair_terms(
        parked, occupied, far_coords, shift_x, shift_y, same_cell
    )
    gain_x, gain_y = apply_rows(k_xx, k_xy, k_yy, far_low)
    totals = (
        forces_x + jnp.sum(pull_x, axis=2),
        forces_y + jnp.sum(pull_y, axis=2),
        push_x + gain_x,
        push_y + gain_y,
        diag_xx + jnp.sum(k_xx.astype(jnp.float32), axis=2),
        diag_xy + jnp.sum(k_xy.astype(jnp.float32), axis=2),
        diag_yy + jnp.sum(k_yy.astype(jnp.float32), axis=2),
    )
    return (totals, (pull_x, pull_y, k_xx, k_xy, k_yy))


def evaluate(coords, occupied, small_q):
    cell_total = coords.shape[0]
    low = small_q.astype(jnp.bfloat16)
    parked = jnp.concatenate(
        [coords[:, 0:1] + PARK * (1.0 - occupied)[:, None, :], coords[:, 1:2]], axis=1
    )
    empty_rows = jnp.zeros(occupied.shape, jnp.float32)
    empty_push = jnp.zeros(small_q[:, 0].shape, jnp.float32)
    totals = (empty_rows, empty_rows, empty_push, empty_push, empty_rows, empty_rows, empty_rows)
    far_low = padded(low, (("space", 0),), cell_total)
    far_coords = padded(parked, (("space", 0),), cell_total)
    for side in (-1, 0, 1):
        if side == 0:
            block_low = low
            block_coords = parked
        else:
            begin = (1 + side) * cell_total
            block_low = far_low[begin : begin + cell_total]
            block_coords = far_coords[begin : begin + cell_total]
        for lane in (-1, 0, 1):
            totals, unused = add_pair(
                totals,
                parked,
                occupied,
                jnp.roll(block_coords, -lane, axis=0),
                jnp.roll(block_low, -lane, axis=0),
                8.0 * side,
                16.0 * lane,
                side == 0 and lane == 0,
            )
    forces_x, forces_y, push_x, push_y, diag_xx, diag_xy, diag_yy = totals
    wide_own = low.astype(jnp.float32)
    push_x = push_x - diag_xx[..., None] * wide_own[:, 0] - diag_xy[..., None] * wide_own[:, 1]
    push_y = push_y - diag_xy[..., None] * wide_own[:, 0] - diag_yy[..., None] * wide_own[:, 1]
    forces = jnp.stack([forces_x, forces_y], axis=1)
    pushes = jnp.stack([push_x, push_y], axis=1)
    return (forces, pushes)


def body(positions, momenta, cell_count, tangent):
    cell_total = positions.shape[0]
    slot_count = positions.shape[2]
    block_cols = tangent.shape[3]
    occupied = (
        lax.broadcasted_iota(jnp.int32, (cell_total, slot_count), 1) < cell_count[:, None]
    ).astype(jnp.float32)
    state = tangent * occupied[:, None, :, None]
    coords = positions
    speeds = momenta
    small_q = state[:, 0:2]
    small_p = state[:, 2:4]
    forces, pushes = evaluate(coords, occupied, small_q)
    for step_index in range(STEPS):
        midway_p = speeds + 0.5 * DT * forces
        midway_dp = small_p + 0.5 * DT * pushes
        coords = coords + DT * midway_p
        small_q = small_q + DT * midway_dp
        forces, pushes = evaluate(coords, occupied, small_q)
        speeds = midway_p + 0.5 * DT * forces
        small_p = midway_dp + 0.5 * DT * pushes
    phase = jnp.concatenate([coords, speeds], axis=1)
    final = jnp.concatenate([small_q, small_p], axis=1)
    rows_form = lax.all_to_all(final, "tangent", split_axis=2, concat_axis=3, tiled=True)
    full_width = rows_form.shape[3]
    flat_rows = rows_form.reshape(-1, full_width)
    partial_value = lax.dot_general(
        flat_rows,
        flat_rows,
        (((0,), (0,)), ((), ())),
        precision=HIGH,
        preferred_element_type=jnp.float32,
    )
    gram_scale = 1.0 / (4.0 * slot_count * cell_total * lax.axis_size("space"))
    gram = lax.psum(partial_value, ("space", "tangent"))
    factor = jnp.linalg.cholesky(gram * gram_scale)
    solved = jax.scipy.linalg.solve_triangular(factor, flat_rows.T, lower=True).T
    columns_out = lax.all_to_all(
        solved.reshape(rows_form.shape), "tangent", split_axis=3, concat_axis=2, tiled=True
    )
    log_diag = jnp.log(jnp.diagonal(factor))
    stretch = lax.dynamic_slice_in_dim(log_diag, lax.axis_index("tangent") * block_cols, block_cols)
    return (phase, columns_out, stretch)


def solution(mesh):
    placed = (
        P(("groups", "space"), None, None),
        P(("groups", "space"), None, None),
        P(("groups", "space")),
        P(("groups", "space"), None, None, "tangent"),
    )
    return jax.shard_map(
        body,
        mesh=mesh,
        in_specs=placed,
        out_specs=(
            P(("groups", "space"), None, None),
            P(("groups", "space"), None, None, "tangent"),
            P(("groups", "tangent")),
        ),
        check_vma=False,
    )
```

profile of v0, /device:TPU:1, one launch (start us, length us, event | category | flops | bytes accessed | tf_op | source)
XLA Modules:
  0.0 639.7 jit_solution(17771305510368086692)
XLA Ops:
  86.5 7.0 %collective-permute-done.10 = bf16[2,2,128,256]{3,2,0,1:T(8,128)(2,1)S(1)} collective-permute-done((bf16[2,2,128,256]{3,2,0,1:T(8,128)(2,1)S(1)}, bf16[2,2,128,256]{3,2,0,1:T(8,128)(2,1)S(1)}, u32[]{:S(2)}, u32[]{:S(2)}) %collective-permute-start.10) | collective-permute-done | bytes 262176 | tf_op jit(solution)/shard_map/ppermute | solution.py:19
  105.5 21.8 %all_to_all.33 = f32[2,4,128,256]{3,0,1,2:T(2,128)S(1)} all-to-all(f32[2,4,128,256]{3,0,1,2:T(2,128)S(1)} %copy.18), channel_id=1, replica_groups=mesh['groups'=2,'space'=4,'tangent'=4] {'tangent'}, dimensions={2} | all-to-all | bytes 2097152 | tf_op jit(solution)/shard_map/all_to_all | solution.py:146
  133.8 107.8 %all-reduce.3.cloned.1.call-done = f32[1024,1024]{0,1:T(8,128)} async-done(((f32[1024,1024]{0,1:T(8,128)}), f32[1024,1024]{0,1:T(8,128)}) %all-reduce.3.cloned.1.call-update) | async-done | bytes 4194320 | tf_op jit(solution)/shard_map/psum | solution.py:157
  246.6 5.7 copy.21
  258.7 11.7 %cholesky.187 = f32[128,128]{1,0:T(8,128)S(1)} custom-call(f32[128,128]{1,0:T(8,128)S(1)} %cholesky.514), custom_call_target="Cholesky" | custom-call | tf_op jit(solution)/shard_map/jit(cholesky)/cholesky | solution.py:158
  271.1 9.8 %custom-call.63 = f32[1,128,128]{1,2,0:T(8,128)S(1)} custom-call(f32[1,128,128]{2,1,0:T(8,128)S(1)} %get-tuple-element.432), custom_call_target="InvertDiagBlocksLowerTriangular" | custom-call | tf_op jit(solution)/shard_map/jit(cholesky)/cholesky | solution.py:158
  287.3 11.9 %cholesky.209 = f32[128,128]{1,0:T(8,128)S(1)} custom-call(f32[128,128]{1,0:T(8,128)S(1)} %cholesky.518), custom_call_target="Cholesky" | custom-call | tf_op jit(solution)/shard_map/jit(cholesky)/cholesky | solution.py:158
  300.5 9.8 %custom-call.64 = f32[1,128,128]{1,2,0:T(8,128)S(1)} custom-call(f32[1,128,128]{2,1,0:T(8,128)S(1)} %get-tuple-element.429), custom_call_target="InvertDiagBlocksLowerTriangular" | custom-call | tf_op jit(solution)/shard_map/jit(cholesky)/cholesky | solution.py:158
  313.6 11.7 %cholesky.402 = f32[128,128]{1,0:T(8,128)S(1)} custom-call(f32[128,128]{1,0:T(8,128)S(1)} %cholesky.523), custom_call_target="Cholesky" | custom-call | tf_op jit(solution)/shard_map/jit(cholesky)/cholesky | solution.py:158
  326.6 9.8 %custom-call.65 = f32[1,128,128]{1,2,0:T(8,128)S(1)} custom-call(f32[1,128,128]{2,1,0:T(8,128)S(1)} %get-tuple-element.426), custom_call_target="InvertDiagBlocksLowerTriangular" | custom-call | tf_op jit(solution)/shard_map/jit(cholesky)/cholesky | solution.py:158
  340.0 11.9 %cholesky.421 = f32[128,128]{1,0:T(8,128)S(1)} custom-call(f32[128,128]{1,0:T(8,128)S(1)} %cholesky.528), custom_call_target="Cholesky" | custom-call | tf_op jit(solution)/shard_map/jit(cholesky)/cholesky | solution.py:158
  353.3 9.8 %custom-call.66 = f32[1,128,128]{1,2,0:T(8,128)S(1)} custom-call(f32[1,128,128]{2,1,0:T(8,128)S(1)} %get-tuple-element.423), custom_call_target="InvertDiagBlocksLowerTriangular" | custom-call | tf_op jit(solution)/shard_map/jit(cholesky)/cholesky | solution.py:158
  366.5 11.7 %cholesky.440 = f32[128,128]{1,0:T(8,128)S(1)} custom-call(f32[128,128]{1,0:T(8,128)S(1)} %cholesky.533), custom_call_target="Cholesky" | custom-call | tf_op jit(solution)/shard_map/jit(cholesky)/cholesky | solution.py:158
  379.6 10.2 %custom-call.67 = f32[1,128,128]{1,2,0:T(8,128)S(1)} custom-call(f32[1,128,128]{2,1,0:T(8,128)S(1)} %get-tuple-element.420), custom_call_target="InvertDiagBlocksLowerTriangular" | custom-call | tf_op jit(solution)/shard_map/jit(cholesky)/cholesky | solution.py:158
  393.1 11.7 %cholesky.460 = f32[128,128]{1,0:T(8,128)S(1)} custom-call(f32[128,128]{1,0:T(8,128)S(1)} %cholesky.538), custom_call_target="Cholesky" | custom-call | tf_op jit(solution)/shard_map/jit(cholesky)/cholesky | solution.py:158
  406.1 9.8 %custom-call.68 = f32[1,128,128]{1,2,0:T(8,128)S(1)} custom-call(f32[1,128,128]{2,1,0:T(8,128)S(1)} %get-tuple-element.417), custom_call_target="InvertDiagBlocksLowerTriangular" | custom-call | tf_op jit(solution)/shard_map/jit(cholesky)/cholesky | solution.py:158
  418.9 11.9 %cholesky.480 = f32[128,128]{1,0:T(8,128)S(1)} custom-call(f32[128,128]{1,0:T(8,128)S(1)} %cholesky.543), custom_call_target="Cholesky" | custom-call | tf_op jit(solution)/shard_map/jit(cholesky)/cholesky | solution.py:158
  432.1 9.8 %custom-call.69 = f32[1,128,128]{1,2,0:T(8,128)S(1)} custom-call(f32[1,128,128]{2,1,0:T(8,128)S(1)} %get-tuple-element.414), custom_call_target="InvertDiagBlocksLowerTriangular" | custom-call | tf_op jit(solution)/shard_map/jit(cholesky)/cholesky | solution.py:158
  444.5 11.7 %cholesky.498 = f32[128,128]{1,0:T(8,128)S(1)} custom-call(f32[128,128]{1,0:T(8,128)S(1)} %convolution_subtract_fusion.13), custom_call_target="Cholesky" | custom-call | tf_op jit(solution)/shard_map/jit(cholesky)/cholesky | solution.py:158
  462.6 6.6 %fusion.1 = (f32[1024,1024]{1,0:T(8,128)}, f32[1024,1024]{1,0:T(8,128)}) fusion(f32[1024,1024]{1,0:T(8,128)} %get-tuple-element.412, pred[]{:T(512)S(6)} %cholesky.513), kind=kLoop, calls=%fused_computation.7 | loop fusion | flops 4194304 | bytes 12582913 | tf_op jit(solution)/shard_map/jit(_solve_triangular)/triangular_solve | solution.py:159
  469.2 23.2 %while.1 = (s32[]{:T(128)}, f32[1024,1024]{1,0:T(8,128)}, s32[8,2]{0,1:T(2,128)S(1)}, f32[8,128,128]{2,1,0:T(8,128)S(1)}, s32[]{:T(128)}) while((s32[]{:T(128)}, f32[1024,1024]{1,0:T(8,128)}, s32[8,2]{0,1:T(2,128)S(1)}, f32[8,128,128]{2,1,0:T(8,128)S(1)}, s32[]{:T(128)}) %tuple.396), condition=%wide.while_cond, body=%wide.while_body.sunk | while | flops 2 | bytes 131189 | solution.py:159
  492.4 79.4 %custom-call.70 = f32[8,128,128]{1,2,0:T(8,128)} custom-call(f32[8,128,128]{2,1,0:T(8,128)S(1)} %get-tuple-element.10), custom_call_target="InvertDiagBlocksLowerTriangular" | custom-call | tf_op jit(solution)/shard_map/jit(_solve_triangular)/triangular_solve | solution.py:159
  595.5 5.5 all-to-all-start.1
  601.7 17.3 %gather_fusion = f32[1024]{0:T(1024)S(1)} fusion(f32[1024,1024]{1,0:T(8,128)} %get-tuple-element.320, s32[1024]{0:T(1024)S(1)} %bitcast.397), kind=kCustom, calls=%fused_computation | custom fusion | bytes 16384 | tf_op jit(solution)/shard_map/jit(diagonal)/cond/branch_0_fun/gather | solution.py:163
  (326 shorter events, 204.9 us)
Async XLA Ops:
  7.2 234.4 %all-reduce.3.cloned.1.call-start = ((), (), s32[]{:S(2)}) async-start(), calls=%async_computation.2 | async-start | bytes 8388608 | tf_op jit(solution)/shard_map/psum | solution.py:157
  8.1 12.2 %collective-permute-start.1 = (f32[2,2,128]{2,1,0:T(2,128)S(1)}, f32[2,2,128]{2,1,0:T(2,128)S(1)}, u32[]{:S(2)}, u32[]{:S(2)}) collective-permute-start(f32[2,2,128]{2,1,0:T(2,128)S(1)} %pad_maximum_fusion.11), channel_id=1, source_target_pairs={{4,0},{8,4},{12,8},{0,12},{5,1},{9,5},{13,9},{1,13},{6,2},{10,6},{... | collective-permute-start | bytes 6152 | tf_op jit(solution)/shard_map/ppermute | solution.py:22
  12.3 8.1 %collective-permute-start = (f32[2,2,128]{2,1,0:T(2,128)S(1)}, f32[2,2,128]{2,1,0:T(2,128)S(1)}, u32[]{:S(2)}, u32[]{:S(2)}) collective-permute-start(f32[2,2,128]{2,1,0:T(2,128)S(1)} %pad_maximum_fusion.11), channel_id=1, source_target_pairs={{0,4},{4,8},{8,12},{12,0},{1,5},{5,9},{9,13},{13,1},{2,6},{6,10},{... | collective-permute-start | bytes 6152 | tf_op jit(solution)/shard_map/ppermute | solution.py:19
  14.4 28.2 %collective-permute-start.7 = (bf16[2,2,128,256]{3,2,0,1:T(8,128)(2,1)S(1)}, bf16[2,2,128,256]{3,2,0,1:T(8,128)(2,1)S(1)}, u32[]{:S(2)}, u32[]{:S(2)}) collective-permute-start(bf16[2,2,128,256]{3,2,0,1:T(8,128)(2,1)S(1)} %get-tuple-element.327), channel_id=1, source_target_pairs={{4,0},{8,4},{12,8},{0,12},{5,1},{9,5},{13,9},{1,13},{6,2},{10,6},{... | collective-permute-start | bytes 786440 | tf_op jit(solution)/shard_map/ppermute | solution.py:22
  17.7 26.6 %collective-permute-start.6 = (bf16[2,2,128,256]{3,2,0,1:T(8,128)(2,1)S(1)}, bf16[2,2,128,256]{3,2,0,1:T(8,128)(2,1)S(1)}, u32[]{:S(2)}, u32[]{:S(2)}) collective-permute-start(bf16[2,2,128,256]{3,2,0,1:T(8,128)(2,1)S(1)} %get-tuple-element.327), channel_id=1, source_target_pairs={{0,4},{4,8},{8,12},{12,0},{1,5},{5,9},{9,13},{13,1},{2,6},{6,10},{... | collective-permute-start | bytes 786440 | tf_op jit(solution)/shard_map/ppermute | solution.py:19
  18.6 4.9 copy-start.3
  18.6 4.9 copy-start.4
  18.7 4.9 copy-start.2
  23.7 4.2 collective-permute-start.3
  27.0 4.2 collective-permute-start.2
  34.6 2.5 collective-permute-start.5
  35.0 4.2 collective-permute-start.4
  57.1 7.5 %collective-permute-start.9 = (bf16[2,2,128,256]{3,2,0,1:T(8,128)(2,1)S(1)}, bf16[2,2,128,256]{3,2,0,1:T(8,128)(2,1)S(1)}, u32[]{:S(2)}, u32[]{:S(2)}) collective-permute-start(bf16[2,2,128,256]{3,2,0,1:T(8,128)(2,1)S(1)} %get-tuple-element.325), channel_id=1, source_target_pairs={{4,0},{8,4},{12,8},{0,12},{5,1},{9,5},{13,9},{1,13},{6,2},{10,6},{... | collective-permute-start | bytes 786440 | tf_op jit(solution)/shard_map/ppermute | solution.py:22
  58.0 8.5 %collective-permute-start.8 = (bf16[2,2,128,256]{3,2,0,1:T(8,128)(2,1)S(1)}, bf16[2,2,128,256]{3,2,0,1:T(8,128)(2,1)S(1)}, u32[]{:S(2)}, u32[]{:S(2)}) collective-permute-start(bf16[2,2,128,256]{3,2,0,1:T(8,128)(2,1)S(1)} %get-tuple-element.325), channel_id=1, source_target_pairs={{0,4},{4,8},{8,12},{12,0},{1,5},{5,9},{9,13},{13,1},{2,6},{6,10},{... | collective-permute-start | bytes 786440 | tf_op jit(solution)/shard_map/ppermute | solution.py:19
  79.4 5.5 collective-permute-start.11
  80.8 12.8 %collective-permute-start.10 = (bf16[2,2,128,256]{3,2,0,1:T(8,128)(2,1)S(1)}, bf16[2,2,128,256]{3,2,0,1:T(8,128)(2,1)S(1)}, u32[]{:S(2)}, u32[]{:S(2)}) collective-permute-start(bf16[2,2,128,256]{3,2,0,1:T(8,128)(2,1)S(1)} %get-tuple-element.322), channel_id=1, source_target_pairs={{0,4},{4,8},{8,12},{12,0},{1,5},{5,9},{9,13},{13,1},{2,6},{6,10},{... | collective-permute-start | bytes 786440 | tf_op jit(solution)/shard_map/ppermute | solution.py:19
  256.8 1.9 copy-start
  571.8 7.2 %copy-start.1 = (f32[8,128,128]{1,2,0:T(8,128)S(1)}, f32[8,128,128]{1,2,0:T(8,128)}, u32[]{:S(2)}) copy-start(f32[8,128,128]{1,2,0:T(8,128)} %custom-call.70) | copy-start | bytes 1572868
  595.5 24.2 %all-to-all-start.1 = ((f32[4,1,65536]{2,1,0:T(1,128)}), f32[4,1,65536]{2,1,0:T(1,128)S(1)}, u32[]{:S(2)}, u32[]{:S(2)}) async-start(f32[4,1,65536]{2,1,0:T(1,128)} %reshape.847), calls=%async_computation.1 | async-start | bytes 2097152 | tf_op jit(solution)/shard_map/all_to_all | solution.py:160
Sparse Core Ops, SparseCore 0:
  133.6 107.9 all-reduce.2
where the time goes:
time: 647 us; the launch traced here: 640 us
  other arithmetic  287 us (44%)
  waiting for transfers between devices  130 us (20%)
  matrix products  87.6 us (14%)
  local copies, waits for them, and re-layouts  71.5 us (11%)
  starting transfers between devices  21.9 us (3%)
  blocking collectives  21.8 us (3%)
  between operations  20.3 us (3%)
    another operation x31, other arithmetic, body(): factor = jnp.linalg.cholesky(gram * gram_scale)  173 us
    psum x1, waiting for transfers between devices, body(): gram = lax.psum(partial_value, ('space', 'tangent'))  108 us
    another operation x3, other arithmetic, body(): jax.scipy.linalg.solve_triangular(factor, flat_rows.T, lower=True)  86 us
    another operation x14, matrix products, body(): factor = jnp.linalg.cholesky(gram * gram_scale)  23.1 us
    another operation x24, local copies, waits for them, and re-layouts  23 us
    all_to_all x1, blocking collectives, body(): lax.all_to_all(final, 'tangent', split_axis=2, concat_axis=3, tiled=True)  21.8 us
    gather x1, local copies, waits for them, and re-layouts, body(): log_diag = jnp.log(jnp.diagonal(factor))  17.3 us
    another operation x15, matrix products, body(): jax.scipy.linalg.solve_triangular(factor, flat_rows.T, lower=True)  14.7 us
  transfers between devices with their start and end apart: 14, of which 9 were waited for; matrix products, arithmetic and copies ran while one was open for 6% of the time, Pallas kernels for 0%

commit v1 on v0

--- a/solution.py
+++ b/solution.py
@@ -157,8 +157,15 @@
     gram = lax.psum(partial_value, ("space", "tangent"))
     factor = jnp.linalg.cholesky(gram * gram_scale)
     solved = jax.scipy.linalg.solve_triangular(factor, flat_rows.T, lower=True).T
-    columns_out = lax.all_to_all(
-        solved.reshape(rows_form.shape), "tangent", split_axis=3, concat_axis=2, tiled=True
+    vec = solved.reshape(rows_form.shape)
+    columns_out = jnp.concatenate(
+        lax.all_to_all(
+            jnp.stack(jnp.split(vec, lax.axis_size("tangent"), 3)),
+            "tangent",
+            split_axis=0,
+            concat_axis=0,
+        ),
+        2,
     )
     log_diag = jnp.log(jnp.diagonal(factor))
     stretch = lax.dynamic_slice_in_dim(log_diag, lax.axis_index("tangent") * block_cols, block_cols)

time: 647 us -> 627 us (0.969)
  local copies, waits for them, and re-layouts: 71.5 us -> 54.2 us
    unnamed x13 -> x11, local copies, waits for them, and re-layouts: 11.7 us -> 2.14 us
    another operation x24 -> x25, local copies, waits for them, and re-layouts: 23 us -> 23.2 us
where the time goes in v1:
time: 627 us; the launch traced here: 620 us
  other arithmetic  285 us (45%)
  waiting for transfers between devices  129 us (21%)
  matrix products  87.6 us (14%)
  local copies, waits for them, and re-layouts  54.2 us (9%)
  blocking collectives  21.8 us (3%)
  starting transfers between devices  21.6 us (3%)
  between operations  20.3 us (3%)
    another operation x31, other arithmetic, body(): factor = jnp.linalg.cholesky(gram * gram_scale)  173 us
    psum x1, waiting for transfers between devices, body(): gram = lax.psum(partial_value, ('space', 'tangent'))  108 us
    another operation x3, other arithmetic, body(): jax.scipy.linalg.solve_triangular(factor, flat_rows.T, lower=True)  86 us
    another operation x14, matrix products, body(): factor = jnp.linalg.cholesky(gram * gram_scale)  23.1 us
    another operation x24, local copies, waits for them, and re-layouts  23 us
    all_to_all x1, blocking collectives, body(): lax.all_to_all(final, 'tangent', split_axis=2, concat_axis=3, tiled=True)  21.8 us
    gather x1, local copies, waits for them, and re-layouts, body(): log_diag = jnp.log(jnp.diagonal(factor))  16.8 us
    another operation x15, matrix products, body(): jax.scipy.linalg.solve_triangular(factor, flat_rows.T, lower=True)  14.7 us
  transfers between devices with their start and end apart: 14, of which 9 were waited for; matrix products, arithmetic and copies ran while one was open for 6% of the time, Pallas kernels for 0%

profile of v1, /device:TPU:1, one launch (start us, length us, event | category | flops | bytes accessed | tf_op | source)
XLA Modules:
  0.0 619.7 jit_solution(3885132230414479871)
XLA Ops:
  86.7 7.0 %collective-permute-done.10 = bf16[2,2,128,256]{3,2,0,1:T(8,128)(2,1)S(1)} collective-permute-done((bf16[2,2,128,256]{3,2,0,1:T(8,128)(2,1)S(1)}, bf16[2,2,128,256]{3,2,0,1:T(8,128)(2,1)S(1)}, u32[]{:S(2)}, u32[]{:S(2)}) %collective-permute-start.10) | collective-permute-done | bytes 262176 | tf_op jit(solution)/shard_map/ppermute | solution.py:19
  105.7 21.8 %all_to_all.20 = f32[2,4,128,256]{3,0,1,2:T(2,128)S(1)} all-to-all(f32[2,4,128,256]{3,0,1,2:T(2,128)S(1)} %copy.24), channel_id=1, replica_groups=mesh['groups'=2,'space'=4,'tangent'=4] {'tangent'}, dimensions={2} | all-to-all | bytes 2097152 | tf_op jit(solution)/shard_map/all_to_all | solution.py:146
  133.9 107.7 %all-reduce.3.cloned.1.call-done = f32[1024,1024]{0,1:T(8,128)} async-done(((f32[1024,1024]{0,1:T(8,128)}), f32[1024,1024]{0,1:T(8,128)}) %all-reduce.3.cloned.1.call-update) | async-done | bytes 4194320 | tf_op jit(solution)/shard_map/psum | solution.py:157
  246.7 5.5 copy.27
  258.6 11.7 %cholesky.187 = f32[128,128]{1,0:T(8,128)S(1)} custom-call(f32[128,128]{1,0:T(8,128)S(1)} %cholesky.514), custom_call_target="Cholesky" | custom-call | tf_op jit(solution)/shard_map/jit(cholesky)/cholesky | solution.py:158
  271.0 9.8 %custom-call.63 = f32[1,128,128]{1,2,0:T(8,128)S(1)} custom-call(f32[1,128,128]{2,1,0:T(8,128)S(1)} %get-tuple-element.436), custom_call_target="InvertDiagBlocksLowerTriangular" | custom-call | tf_op jit(solution)/shard_map/jit(cholesky)/cholesky | solution.py:158
  287.2 11.9 %cholesky.209 = f32[128,128]{1,0:T(8,128)S(1)} custom-call(f32[128,128]{1,0:T(8,128)S(1)} %cholesky.518), custom_call_target="Cholesky" | custom-call | tf_op jit(solution)/shard_map/jit(cholesky)/cholesky | solution.py:158
  300.4 9.8 %custom-call.64 = f32[1,128,128]{1,2,0:T(8,128)S(1)} custom-call(f32[1,128,128]{2,1,0:T(8,128)S(1)} %get-tuple-element.433), custom_call_target="InvertDiagBlocksLowerTriangular" | custom-call | tf_op jit(solution)/shard_map/jit(cholesky)/cholesky | solution.py:158
  313.5 11.7 %cholesky.402 = f32[128,128]{1,0:T(8,128)S(1)} custom-call(f32[128,128]{1,0:T(8,128)S(1)} %cholesky.523), custom_call_target="Cholesky" | custom-call | tf_op jit(solution)/shard_map/jit(cholesky)/cholesky | solution.py:158
  326.5 9.8 %custom-call.65 = f32[1,128,128]{1,2,0:T(8,128)S(1)} custom-call(f32[1,128,128]{2,1,0:T(8,128)S(1)} %get-tuple-element.430), custom_call_target="InvertDiagBlocksLowerTriangular" | custom-call | tf_op jit(solution)/shard_map/jit(cholesky)/cholesky | solution.py:158
  339.9 12.1 %cholesky.421 = f32[128,128]{1,0:T(8,128)S(1)} custom-call(f32[128,128]{1,0:T(8,128)S(1)} %cholesky.528), custom_call_target="Cholesky" | custom-call | tf_op jit(solution)/shard_map/jit(cholesky)/cholesky | solution.py:158
  353.4 9.8 %custom-call.66 = f32[1,128,128]{1,2,0:T(8,128)S(1)} custom-call(f32[1,128,128]{2,1,0:T(8,128)S(1)} %get-tuple-element.427), custom_call_target="InvertDiagBlocksLowerTriangular" | custom-call | tf_op jit(solution)/shard_map/jit(cholesky)/cholesky | solution.py:158
  366.6 11.7 %cholesky.440 = f32[128,128]{1,0:T(8,128)S(1)} custom-call(f32[128,128]{1,0:T(8,128)S(1)} %cholesky.533), custom_call_target="Cholesky" | custom-call | tf_op jit(solution)/shard_map/jit(cholesky)/cholesky | solution.py:158
  379.7 10.0 %custom-call.67 = f32[1,128,128]{1,2,0:T(8,128)S(1)} custom-call(f32[1,128,128]{2,1,0:T(8,128)S(1)} %get-tuple-element.424), custom_call_target="InvertDiagBlocksLowerTriangular" | custom-call | tf_op jit(solution)/shard_map/jit(cholesky)/cholesky | solution.py:158
  393.0 11.7 %cholesky.460 = f32[128,128]{1,0:T(8,128)S(1)} custom-call(f32[128,128]{1,0:T(8,128)S(1)} %cholesky.538), custom_call_target="Cholesky" | custom-call | tf_op jit(solution)/shard_map/jit(cholesky)/cholesky | solution.py:158
  406.0 9.8 %custom-call.68 = f32[1,128,128]{1,2,0:T(8,128)S(1)} custom-call(f32[1,128,128]{2,1,0:T(8,128)S(1)} %get-tuple-element.421), custom_call_target="InvertDiagBlocksLowerTriangular" | custom-call | tf_op jit(solution)/shard_map/jit(cholesky)/cholesky | solution.py:158
  418.8 11.9 %cholesky.480 = f32[128,128]{1,0:T(8,128)S(1)} custom-call(f32[128,128]{1,0:T(8,128)S(1)} %cholesky.543), custom_call_target="Cholesky" | custom-call | tf_op jit(solution)/shard_map/jit(cholesky)/cholesky | solution.py:158
  432.0 9.8 %custom-call.69 = f32[1,128,128]{1,2,0:T(8,128)S(1)} custom-call(f32[1,128,128]{2,1,0:T(8,128)S(1)} %get-tuple-element.418), custom_call_target="InvertDiagBlocksLowerTriangular" | custom-call | tf_op jit(solution)/shard_map/jit(cholesky)/cholesky | solution.py:158
  444.4 11.7 %cholesky.498 = f32[128,128]{1,0:T(8,128)S(1)} custom-call(f32[128,128]{1,0:T(8,128)S(1)} %convolution_subtract_fusion.13), custom_call_target="Cholesky" | custom-call | tf_op jit(solution)/shard_map/jit(cholesky)/cholesky | solution.py:158
  462.5 6.6 %fusion.1 = (f32[1024,1024]{1,0:T(8,128)}, f32[1024,1024]{1,0:T(8,128)}) fusion(f32[1024,1024]{1,0:T(8,128)} %get-tuple-element.416, pred[]{:T(512)S(6)} %cholesky.513), kind=kLoop, calls=%fused_computation.7 | loop fusion | flops 4194304 | bytes 12582913 | tf_op jit(solution)/shard_map/jit(_solve_triangular)/triangular_solve | solution.py:159
  469.1 23.2 %while.1 = (s32[]{:T(128)}, f32[1024,1024]{1,0:T(8,128)}, s32[8,2]{0,1:T(2,128)S(1)}, f32[8,128,128]{2,1,0:T(8,128)S(1)}, s32[]{:T(128)}) while((s32[]{:T(128)}, f32[1024,1024]{1,0:T(8,128)}, s32[8,2]{0,1:T(2,128)S(1)}, f32[8,128,128]{2,1,0:T(8,128)S(1)}, s32[]{:T(128)}) %tuple.399), condition=%wide.while_cond, body=%wide.while_body.sunk | while | flops 2 | bytes 131189 | solution.py:159
  492.3 79.5 %custom-call.70 = f32[8,128,128]{1,2,0:T(8,128)} custom-call(f32[8,128,128]{2,1,0:T(8,128)S(1)} %get-tuple-element.10), custom_call_target="InvertDiagBlocksLowerTriangular" | custom-call | tf_op jit(solution)/shard_map/jit(_solve_triangular)/triangular_solve | solution.py:159
  588.1 5.3 all-to-all-start.1
  594.1 16.8 %gather_fusion = f32[1024]{0:T(1024)S(1)} fusion(f32[1024,1024]{1,0:T(8,128)} %get-tuple-element.320, s32[1024]{0:T(1024)S(1)} %bitcast.401), kind=kCustom, calls=%fused_computation | custom fusion | bytes 16384 | tf_op jit(solution)/shard_map/jit(diagonal)/cond/branch_0_fun/gather | solution.py:170
  (323 shorter events, 185.8 us)
Async XLA Ops:
  7.2 234.5 %all-reduce.3.cloned.1.call-start = ((), (), s32[]{:S(2)}) async-start(), calls=%async_computation.2 | async-start | bytes 8388608 | tf_op jit(solution)/shard_map/psum | solution.py:157
  8.1 12.2 %collective-permute-start.1 = (f32[2,2,128]{2,1,0:T(2,128)S(1)}, f32[2,2,128]{2,1,0:T(2,128)S(1)}, u32[]{:S(2)}, u32[]{:S(2)}) collective-permute-start(f32[2,2,128]{2,1,0:T(2,128)S(1)} %pad_maximum_fusion.12), channel_id=1, source_target_pairs={{4,0},{8,4},{12,8},{0,12},{5,1},{9,5},{13,9},{1,13},{6,2},{10,6},{... | collective-permute-start | bytes 6152 | tf_op jit(solution)/shard_map/ppermute | solution.py:22
  12.3 8.1 %collective-permute-start = (f32[2,2,128]{2,1,0:T(2,128)S(1)}, f32[2,2,128]{2,1,0:T(2,128)S(1)}, u32[]{:S(2)}, u32[]{:S(2)}) collective-permute-start(f32[2,2,128]{2,1,0:T(2,128)S(1)} %pad_maximum_fusion.12), channel_id=1, source_target_pairs={{0,4},{4,8},{8,12},{12,0},{1,5},{5,9},{9,13},{13,1},{2,6},{6,10},{... | collective-permute-start | bytes 6152 | tf_op jit(solution)/shard_map/ppermute | solution.py:19
  14.4 28.6 %collective-permute-start.7 = (bf16[2,2,128,256]{3,2,0,1:T(8,128)(2,1)S(1)}, bf16[2,2,128,256]{3,2,0,1:T(8,128)(2,1)S(1)}, u32[]{:S(2)}, u32[]{:S(2)}) collective-permute-start(bf16[2,2,128,256]{3,2,0,1:T(8,128)(2,1)S(1)} %get-tuple-element.327), channel_id=1, source_target_pairs={{4,0},{8,4},{12,8},{0,12},{5,1},{9,5},{13,9},{1,13},{6,2},{10,6},{... | collective-permute-start | bytes 786440 | tf_op jit(solution)/shard_map/ppermute | solution.py:22
  17.7 26.9 %collective-permute-start.6 = (bf16[2,2,128,256]{3,2,0,1:T(8,128)(2,1)S(1)}, bf16[2,2,128,256]{3,2,0,1:T(8,128)(2,1)S(1)}, u32[]{:S(2)}, u32[]{:S(2)}) collective-permute-start(bf16[2,2,128,256]{3,2,0,1:T(8,128)(2,1)S(1)} %get-tuple-element.327), channel_id=1, source_target_pairs={{0,4},{4,8},{8,12},{12,0},{1,5},{5,9},{9,13},{13,1},{2,6},{6,10},{... | collective-permute-start | bytes 786440 | tf_op jit(solution)/shard_map/ppermute | solution.py:19
  18.6 4.9 copy-start.3
  18.6 4.9 copy-start.4
  18.7 4.9 copy-start.2
  23.7 4.2 collective-permute-start.3
  27.0 4.2 collective-permute-start.2
  34.6 2.5 collective-permute-start.5
  35.0 4.2 collective-permute-start.4
  57.4 7.3 %collective-permute-start.9 = (bf16[2,2,128,256]{3,2,0,1:T(8,128)(2,1)S(1)}, bf16[2,2,128,256]{3,2,0,1:T(8,128)(2,1)S(1)}, u32[]{:S(2)}, u32[]{:S(2)}) collective-permute-start(bf16[2,2,128,256]{3,2,0,1:T(8,128)(2,1)S(1)} %get-tuple-element.325), channel_id=1, source_target_pairs={{4,0},{8,4},{12,8},{0,12},{5,1},{9,5},{13,9},{1,13},{6,2},{10,6},{... | collective-permute-start | bytes 786440 | tf_op jit(solution)/shard_map/ppermute | solution.py:22
  58.1 8.5 %collective-permute-start.8 = (bf16[2,2,128,256]{3,2,0,1:T(8,128)(2,1)S(1)}, bf16[2,2,128,256]{3,2,0,1:T(8,128)(2,1)S(1)}, u32[]{:S(2)}, u32[]{:S(2)}) collective-permute-start(bf16[2,2,128,256]{3,2,0,1:T(8,128)(2,1)S(1)} %get-tuple-element.325), channel_id=1, source_target_pairs={{0,4},{4,8},{8,12},{12,0},{1,5},{5,9},{9,13},{13,1},{2,6},{6,10},{... | collective-permute-start | bytes 786440 | tf_op jit(solution)/shard_map/ppermute | solution.py:19
  79.5 5.5 collective-permute-start.11
  80.9 12.8 %collective-permute-start.10 = (bf16[2,2,128,256]{3,2,0,1:T(8,128)(2,1)S(1)}, bf16[2,2,128,256]{3,2,0,1:T(8,128)(2,1)S(1)}, u32[]{:S(2)}, u32[]{:S(2)}) collective-permute-start(bf16[2,2,128,256]{3,2,0,1:T(8,128)(2,1)S(1)} %get-tuple-element.322), channel_id=1, source_target_pairs={{0,4},{4,8},{8,12},{12,0},{1,5},{5,9},{9,13},{13,1},{2,6},{6,10},{... | collective-permute-start | bytes 786440 | tf_op jit(solution)/shard_map/ppermute | solution.py:19
  256.6 1.9 copy-start
  571.7 7.2 %copy-start.1 = (f32[8,128,128]{1,2,0:T(8,128)S(1)}, f32[8,128,128]{1,2,0:T(8,128)}, u32[]{:S(2)}) copy-start(f32[8,128,128]{1,2,0:T(8,128)} %custom-call.70) | copy-start | bytes 1572868
  588.1 23.4 %all-to-all-start.1 = ((f32[4,2,4,32,256]{4,3,2,1,0:T(8,128)}), f32[4,2,4,32,256]{4,3,2,1,0:T(8,128)S(1)}, u32[]{:S(2)}, u32[]{:S(2)}) async-start(f32[4,2,4,32,256]{4,3,2,1,0:T(8,128)} %pad_maximum_fusion.1), calls=%async_computation.1 | async-start | bytes 2097152 | tf_op jit(solution)/shard_map/all_to_all | solution.py:162
Sparse Core Ops, SparseCore 0:
  133.7 107.9 all-reduce.2
